TPU v7x, 32 devices: a whole 2x2x4 slice. The times are simulated.
32 devices in a mesh: groups: 2 (over x), pairs: 16 (over z, y, core).
Axes of the slice: x: 2, y: 2, z: 4, core: 2. Of those that a mesh axis runs over, the one named last changes fastest.
Arguments:
- traces: bfloat16 [128, 3, 4096], P(('groups', 'pairs')), parts along dimension 0, may hold values from -6 to 6
- gaps: int32 [128, 2], P(('groups', 'pairs')), parts along dimension 0, may hold values 0 or 1
- assign: int32 [128], P('groups'), parts along dimension 0, may hold values from 0 to 3, as said below
- target: int32 [32], P('groups'), parts along dimension 0, may hold values from 0 to 3, as said below
Outputs:
- correlations: bfloat16 [128, 16, 2, 9, 256], P(('groups', 'pairs')), parts along dimension 0
- energy: float32 [128, 9], P(('groups', 'pairs')), parts along dimension 0
There are 2 independent parts, one for each index of `groups`. A program takes and returns all parts, laid end to end along the dimension named above; each array names one. Nothing has to cross between parts.
Inputs may be any that keep to these rules, and one draw needn't show every extreme that they name: `assign`: the 4 stations of one owner name at most 2 stations of any block; in every draw one block takes exactly 2 stations of every owner. `target`: in every draw some owner names the block that takes 2 stations of every owner.
All inputs are finite; a program needn't handle non-finite values. No bound on the sum of `gaps` on one device may be relied on, other than what follows from the above.
Results may differ from a plain program's by a relative error of at most 0.0075.
Values may be sent and summed in bfloat16 or wider, within the bound.
A program may use at most 128 MiB of HBM per device.

v0:
```python
import math

import jax
import jax.numpy as jnp
from jax import lax
from jax.sharding import PartitionSpec as P

SEG = 2048
FREQ = 512
FLO = 64
LAGS = 256
HALF = 21
CAP = 2


def dft_table():
    samples = jnp.arange(SEG, dtype=jnp.int32)[:, None]
    bins = FLO + jnp.arange(FREQ, dtype=jnp.int32)[None, :]
    phase = jnp.mod(samples * bins, SEG).astype(jnp.float32) * (2.0 * math.pi / SEG)
    return jnp.concatenate([jnp.cos(phase), -jnp.sin(phase)], axis=1).astype(jnp.bfloat16)


def lag_table():
    bins = FLO + jnp.arange(FREQ, dtype=jnp.int32)[:, None]
    shifts = jnp.arange(LAGS, dtype=jnp.int32)[None, :] - LAGS // 2
    phase = jnp.mod(bins * shifts, SEG).astype(jnp.float32) * (2.0 * math.pi / SEG)
    return jnp.concatenate([jnp.cos(phase), -jnp.sin(phase)], axis=0).astype(jnp.bfloat16)


def smooth_band():
    column = jnp.arange(FREQ, dtype=jnp.int32)
    band = (jnp.abs(column[:, None] - column[None, :]) <= HALF).astype(jnp.float32)
    return (band, jnp.sum(band, axis=0))


def whiten_all(traces, gaps):
    stations = traces.shape[0]
    windows = gaps.shape[1]
    segments = traces.reshape(stations * 3 * windows, SEG)
    spectra = jnp.dot(segments, dft_table(), preferred_element_type=jnp.float32)
    spectra = spectra.reshape(stations, 3, windows, 2, FREQ)
    power = jnp.sum(spectra * spectra, axis=(1, 3)) / 3.0
    band, bin_count = smooth_band()
    smooth = jnp.dot(power.reshape(-1, FREQ), band, precision=lax.Precision.HIGHEST)
    smooth = smooth.reshape(stations, windows, FREQ) / bin_count
    factor = gaps.astype(jnp.float32)[:, :, None] / jnp.sqrt(smooth + 1e-06)
    return (spectra * factor[:, None, :, None, :]).astype(jnp.bfloat16)


def station_ranks(owner_assign):
    own_count = owner_assign.shape[1]
    same = owner_assign[:, :, None] == owner_assign[:, None, :]
    order = jnp.arange(own_count, dtype=jnp.int32)
    before = order[:, None] < order[None, :]
    return jnp.sum((same & before[None, :, :]).astype(jnp.int32), axis=1)


def correlate_block(whitened, own_mask, partner, partner_mask, lag_tab):
    own_count = whitened.shape[0]
    slot_count = partner.shape[0]
    real_part = partner[:, :, :, 0]
    imag_part = partner[:, :, :, 1]
    quad = jnp.stack(
        [jnp.stack([real_part, imag_part], 3), jnp.stack([-imag_part, real_part], 3)], 4
    )
    cross = jnp.einsum("icwrf,jdwrof->ijcdof", whitened, quad, preferred_element_type=jnp.float32)
    cross = cross.astype(jnp.bfloat16)
    lagged = jnp.dot(cross.reshape(-1, 2 * FREQ), lag_tab, preferred_element_type=jnp.float32)
    lagged = lagged.reshape(own_count, slot_count, 9, LAGS)
    counts = jnp.dot(own_mask, partner_mask.T, precision=lax.Precision.HIGHEST)
    scale = 1.0 / (jnp.maximum(counts, 1.0) * math.sqrt(FREQ))
    return (lagged * scale[:, :, None, None]).astype(jnp.bfloat16)


def correlate_slots(whitened, own_mask, partner, partner_mask):
    own_count = whitened.shape[0]
    windows = whitened.shape[2]
    senders = partner.shape[0]
    width = partner.shape[1]
    stride = min(senders, 16)
    lag_tab = lag_table()
    initial = jnp.zeros((own_count, senders, width, 9, LAGS), jnp.bfloat16)

    def advance(position, filled):
        start = position * stride
        piece = lax.dynamic_slice_in_dim(partner, start, stride, 0)
        piece = piece.reshape(stride * width, 3, windows, 2, FREQ)
        mask_piece = lax.dynamic_slice_in_dim(partner_mask, start, stride, 0)
        mask_piece = mask_piece.reshape(stride * width, windows).astype(jnp.float32)
        result = correlate_block(whitened, own_mask, piece, mask_piece, lag_tab)
        result = result.reshape(own_count, stride, width, 9, LAGS)
        return lax.dynamic_update_slice_in_dim(filled, result, start, 1)

    return lax.fori_loop(0, senders // stride, advance, initial)


def on_device(traces, gaps, assign, target):
    whitened = whiten_all(traces, gaps)
    own_count = whitened.shape[0]
    owners = lax.axis_size("pairs")
    my_index = lax.axis_index("pairs")
    own_mask = gaps.astype(jnp.float32)
    station_rows = whitened.reshape(own_count, -1)
    mask_rows = gaps.astype(jnp.bfloat16)
    owner_assign = assign.reshape(owners, own_count)
    ranks = station_ranks(owner_assign)
    slot_ids = jnp.arange(CAP, dtype=jnp.int32)
    wanted = lax.dynamic_index_in_dim(target, my_index, 0, keepdims=False)
    select_in = (
        (owner_assign == wanted)[:, None, :] & (ranks[:, None, :] == slot_ids[None, :, None])
    ).astype(jnp.bfloat16)
    my_assign = lax.dynamic_index_in_dim(owner_assign, my_index, 0, keepdims=False)
    my_ranks = lax.dynamic_index_in_dim(ranks, my_index, 0, keepdims=False)
    select_out = (
        (my_assign[None, :] == target[:, None])[:, None, :]
        & (my_ranks[None, None, :] == slot_ids[None, :, None])
    ).astype(jnp.bfloat16)
    everyone, every_mask = (
        lax.all_gather(station_rows, "pairs", axis=0, tiled=True),
        lax.all_gather(mask_rows, "pairs", axis=0, tiled=True),
    )
    partner = jnp.einsum(
        "ecs,esr->ecr",
        select_in,
        everyone.reshape(owners, own_count, -1),
        preferred_element_type=jnp.float32,
    ).astype(jnp.bfloat16)
    partner_mask = jnp.einsum(
        "ecs,esw->ecw",
        select_in,
        every_mask.reshape(owners, own_count, -1),
        preferred_element_type=jnp.float32,
    ).astype(jnp.bfloat16)
    correlations = correlate_slots(whitened, own_mask, partner, partner_mask)
    slot_energy = jnp.sum(jnp.square(correlations.astype(jnp.float32)), axis=(0, 4))
    returned = lax.all_to_all(slot_energy, "pairs", split_axis=0, concat_axis=0, tiled=True)
    energy = jnp.einsum(
        "pcs,pcq->sq", select_out.astype(jnp.float32), returned, precision=lax.Precision.HIGHEST
    )
    energy = energy / float(owners * LAGS)
    return (correlations, energy)


def solution(mesh):
    in_specs = (
        P(("groups", "pairs"), None, None),
        P(("groups", "pairs"), None),
        P("groups"),
        P("groups"),
    )
    out_specs = (P(("groups", "pairs"), None, None, None, None), P(("groups", "pairs"), None))
    return jax.shard_map(
        on_device, mesh=mesh, in_specs=in_specs, out_specs=out_specs, check_vma=False
    )
```

profile of v0, /device:TPU:0, one launch (start us, length us, event | category | flops | bytes accessed | tf_op | source)
XLA Modules:
  0.0 122.4 jit_solution(12688342774132318976)
XLA Ops:
  0.7 0.1 convert_reduce_fusion
  0.8 1.0 copy.74
  1.7 0.1 reshape.137
  1.8 17.0 %cosine_convert_fusion = (bf16[2048,512]{1,0:T(8,128)(2,1)S(1)}, bf16[2048,512]{1,0:T(8,128)(2,1)S(1)}) fusion(s32[512]{0:T(512)S(1)} %iota_add_fusion), kind=kLoop, calls=%fused_computation.14 | loop fusion | flops 17825792 | bytes 4196352 | tf_op jit(solution)/shard_map/convert.2
  18.8 0.0 copy-start.1
  18.8 0.0 copy-start.2
  18.9 0.0 copy-start.3
  18.9 0.6 fusion.14
  19.5 0.1 reshape.139
  19.6 0.1 reshape.138
  19.7 0.1 reshape.136
  19.8 0.1 copy.71
  19.9 0.6 dynamic_slice.17
  20.5 0.6 broadcast_compare_fusion
  21.1 0.1 convert_reduce_fusion.1
  21.2 0.1 copy.73
  21.3 0.1 multiply_reduce_fusion.1
  21.4 0.3 fusion.19
  21.8 0.1 mul.96
  22.0 25.5 %all-gather = bf16[16,4,6144]{2,1,0:T(4,128)(2,1)S(1)} all-gather(bf16[1,4,6144]{2,1,0:T(4,128)(2,1)S(1)} %fusion.31), channel_id=1, replica_groups=mesh['groups'=2,'pairs'=16] {'pairs'}, dimensions={0}, use_global_device_ids=true | all-gather | bytes 835584 | tf_op jit(solution)/shard_map/all_gather | solution.py:119
  47.4 0.6 convolution_convert_fusion
  48.0 0.2 reshape.141
  48.3 0.2 stack.20
  48.5 0.5 iota_add_fusion.1
  49.1 17.3 %all-gather.1 = bf16[16,4,2]{1,2,0:T(2,128)(2,1)S(1)} all-gather(bf16[1,4,2]{1,2,0:T(2,128)(2,1)S(1)} %get-tuple-element.44), channel_id=1, replica_groups=mesh['groups'=2,'pairs'=16] {'pairs'}, dimensions={0}, use_global_device_ids=true | all-gather | bytes 272 | tf_op jit(solution)/shard_map/all_gather | solution.py:120
  66.4 0.1 convolution_convert_fusion.1
  66.5 0.8 fusion.22
  67.3 1.7 %copy.88 = bf16[4,3,2,2,512,1,1]{0,2,3,1,6,5,4:T(2,128)(2,1)S(1)} copy(bf16[4,3,2,2,512,1,1]{4,3,2,1,0,6,5:T(2,128)(2,1)S(1)} %fusion.32) | data formatting | bytes 98304 | tf_op jit(solution)/shard_map/convert_element_type | solution.py:47
  69.0 0.5 fusion.48
  69.6 0.1 copy.95
  69.7 0.1 copy_negate_fusion
  69.8 0.8 pad_maximum_fusion
  70.5 3.5 %copy.79 = bf16[32,3,2,2,512]{0,2,3,1,4:T(2,128)(2,1)S(1)} copy(bf16[32,3,2,2,512]{4,0,3,2,1:T(8,128)(2,1)} %pad_maximum_fusion) | data formatting | bytes 786432 | tf_op jit(solution)/shard_map/while/body/eval_jaxpr/stack | solution.py:64
  74.1 3.1 %copy.80 = bf16[32,3,2,2,1,512]{0,2,3,4,1,5:T(2,128)(2,1)} copy(bf16[32,3,2,2,1,512]{5,3,2,1,0,4:T(2,128)(2,1)S(1)} %stack.20) | data formatting | bytes 786432 | tf_op jit(solution)/shard_map/while/body/eval_jaxpr/stack | solution.py:63
  77.2 11.5 %fusion = bf16[4,32,3,3,2,512]{1,0,2,4,3,5:T(4,128)(2,1)} fusion(bf16[4,3,2,2,512,1,1]{0,2,3,1,6,5,4:T(2,128)(2,1)S(1)} %copy.88, bf16[32,3,2,2,1,512]{0,2,3,4,1,5:T(2,128)(2,1)S(1)} %bitcast.54, bf16[32,3,2,2,1,512]{0,2,3,4,1,5:T(2,128)(2,1)} %copy.80), kind=kOutput, calls=%fused_computation.1 | convolution fusion | flops 12189696 | bytes 3194880 | tf_op jit(solution)/shard_map/while/body/eval_jaxpr/icwrf,jdwrof->ijcdof/dot_general | solution.py:66
  88.7 14.3 %copy.82 = bf16[4,32,3,3,2,512]{5,4,1,3,2,0:T(2,128)(2,1)S(1)} copy(bf16[4,32,3,3,2,512]{1,0,2,4,3,5:T(4,128)(2,1)} %fusion) | data formatting | bytes 4718592 | tf_op jit(solution)/shard_map/while/body/eval_jaxpr/convert_element_type | solution.py:67
  103.0 0.0 copy-start.5
  103.0 2.9 %dot_general.36 = bf16[4,32,9,1024]{3,1,2,0:T(8,128)(2,1)} reshape(bf16[4,32,3,3,2,512]{5,4,1,3,2,0:T(2,128)(2,1)S(1)} %copy.82) | data formatting | bytes 4718592 | tf_op jit(solution)/shard_map/while/body/eval_jaxpr/dot_general | solution.py:68
  105.9 2.5 %cosine_convert_fusion.1 = (bf16[512,256]{1,0:T(8,128)(2,1)S(1)}, bf16[512,256]{1,0:T(8,128)(2,1)S(1)}) fusion(s32[256]{0:T(256)S(1)} %copy-done, s32[512]{0:T(512)S(1)} %iota_add_fusion), kind=kLoop, calls=%fused_computation.51 | loop fusion | flops 2228224 | bytes 527360 | tf_op jit(solution)/shard_map/convert
  108.4 2.5 %multiply_reduce_fusion = (f32[32,9]{0,1:T(8,128)S(1)}, bf16[4,32,9,256]{3,1,2,0:T(8,128)(2,1)S(1)}) fusion(f32[4,32]{1,0:T(4,128)S(1)} %copy-done.5, bf16[4,32,9,1024]{3,1,2,0:T(8,128)(2,1)} %dot_general.36, bf16[512,256]{1,0:T(8,128)(2,1)S(1)} %get-tuple-element.41, bf16[512,256]{1,0:T(8,128)(2,1)S(1)} %get-tuple-element.40), kind=kOutput, calls=%fused_computation.23 | convolution fusion | flops 606502656 | bytes 3475072 | tf_op jit(solution)/shard_map/while/body/eval_jaxpr/dot_general | solution.py:68
  110.9 0.7 copy.84
  111.6 3.5 %all-to-all-start = ((f32[16,2,9]{2,1,0:T(2,128)}), f32[16,2,9]{2,1,0:T(2,128)S(1)}, u32[]{:S(2)}, u32[]{:S(2)}) async-start(f32[16,2,9]{2,1,0:T(2,128)} %bitcast.17), calls=%async_computation | async-start | bytes 32768 | tf_op jit(solution)/shard_map/all_to_all | solution.py:136
  115.1 0.2 dynamic-slice_reduce_fusion
  115.3 0.1 broadcast_compare_fusion.1
  115.4 0.2 reshape.144
  115.7 1.2 copy.86
  116.9 4.7 %all-to-all-done = f32[16,2,9]{2,1,0:T(2,128)S(1)} async-done(((f32[16,2,9]{2,1,0:T(2,128)}), f32[16,2,9]{2,1,0:T(2,128)S(1)}, u32[]{:S(2)}, u32[]{:S(2)}) %all-to-all-start) | async-done | bytes 1184 | tf_op jit(solution)/shard_map/all_to_all | solution.py:136
  121.6 0.8 fusion.23
  (17 shorter events, 0.2 us)
Async XLA Ops:
  18.8 0.9 copy-start.1
  18.8 0.9 copy-start.2
  18.9 1.0 copy-start.3
  103.0 2.9 %copy-start = (s32[256]{0:T(256)S(1)}, s32[256]{0:T(256)}, u32[]{:S(2)}) copy-start(s32[256]{0:T(256)} %iota_add_fusion.1) | copy-start | bytes 3076
  103.0 5.4 %copy-start.5 = (f32[4,32]{1,0:T(4,128)S(1)}, f32[4,32]{1,0:T(4,128)}, u32[]{:S(2)}) copy-start(f32[4,32]{1,0:T(4,128)} %fusion.22) | copy-start | bytes 1540
  105.9 9.4 %copy-start.4 = (s32[16]{0:T(128)S(1)}, s32[16]{0:T(128)}, u32[]{:S(2)}) copy-start(s32[16]{0:T(128)} %param.7) | copy-start | bytes 196
  111.6 10.0 %all-to-all-start = ((f32[16,2,9]{2,1,0:T(2,128)}), f32[16,2,9]{2,1,0:T(2,128)S(1)}, u32[]{:S(2)}, u32[]{:S(2)}) async-start(f32[16,2,9]{2,1,0:T(2,128)} %bitcast.17), calls=%async_computation | async-start | bytes 32768 | tf_op jit(solution)/shard_map/all_to_all | solution.py:136
where the time goes:
time: 123 us; the launch traced here: 122 us
  blocking collectives  42.8 us (35%)
  local copies, waits for them, and re-layouts  31.3 us (25%)
  other arithmetic  21.9 us (18%)
  matrix products  17.3 us (14%)
  waiting for transfers between devices  4.72 us (4%)
  starting transfers between devices  3.49 us (3%)
    all_gather x1, blocking collectives, on_device(): lax.all_gather(station_rows, 'pairs', axis=0, tiled=True)  25.5 us
    another operation x2, other arithmetic  19.5 us
    all_gather x1, blocking collectives, on_device(): lax.all_gather(mask_rows, 'pairs', axis=0, tiled=True)  17.3 us
    convert_element_type x1, local copies, waits for them, and re-layouts, correlate_block(): cross = cross.astype(jnp.bfloat16)  14.3 us
    dot_general x1, matrix products, correlate_block(): jnp.einsum('icwrf,jdwrof->ijcdof', whitened, quad, preferred_element_type...  11.5 us
    all_to_all x1, waiting for transfers between devices, on_device(): lax.all_to_all(slot_energy, 'pairs', split_axis=0, concat_axis=0, tiled=T...  4.72 us
    another operation x1, local copies, waits for them, and re-layouts, correlate_block(): jnp.stack([-imag_part, real_part], 3)  3.52 us
    all_to_all x1, starting transfers between devices, on_device(): lax.all_to_all(slot_energy, 'pairs', split_axis=0, concat_axis=0, tiled=T...  3.49 us
  transfers between devices with their start and end apart: 1, of which 1 were waited for; matrix products, arithmetic and copies ran while one was open for 1% of the time, Pallas kernels for 0%

commit v1 on v0

v1 whole, which is shorter than its diff:
```python
import functools
import math

import jax
import jax.numpy as jnp
import numpy as np
from jax import lax
from jax.experimental import pallas as pl
from jax.experimental.pallas import tpu as pltpu
from jax.sharding import PartitionSpec as P

SEG = 2048
FREQ = 512
FLO = 64
LAGS = 256
HALF = 21
CAP = 2
LANE = 128
PLANE = 4


def tables():
    step = np.float32(2.0 * math.pi / SEG)
    bins = FLO + np.arange(FREQ)
    phase = ((np.arange(SEG)[:, None] * bins[None, :]) % SEG).astype(np.float32) * step
    dft = np.concatenate([np.cos(phase), -np.sin(phase)], axis=1)
    shifts = np.arange(LAGS) - LAGS // 2
    phase = ((bins[:, None] * shifts[None, :]) % SEG).astype(np.float32) * step
    lag = np.concatenate([np.cos(phase), -np.sin(phase)], axis=0)
    return jnp.asarray(dft, jnp.bfloat16), jnp.asarray(lag, jnp.bfloat16)


def pick(assign_ref, target_ref, owner, wanted, own):
    block = target_ref[wanted]
    seen = jnp.int32(0)
    slots = [jnp.int32(-1)] * CAP
    for s in range(own):
        hit = (assign_ref[owner * own + s] == block).astype(jnp.int32)
        for c in range(CAP):
            slots[c] = jnp.where(hit * (seen == c).astype(jnp.int32) == 1, s, slots[c])
        seen = seen + hit
    return slots


def kernel(
    owners, own, wins, traces_ref, gaps_ref, assign_ref, target_ref, dft_ref, lag_ref,
    corr_ref, energy_ref,
    gath, ownx, part, cross, lagged, esend, erecv,
    zs, zr, ys, yr, cs, cr, es, er,
):
    me = lax.axis_index("pairs")
    planes = owners // PLANE
    z = me // PLANE
    core = me % 2
    peer = me + 1 - 2 * core
    yy = (me // 2) % 2
    across = me + 2 - 4 * yy
    f32, bf16 = jnp.float32, jnp.bfloat16
    rows = 2 * 3 * wins * own
    grp = own * CAP
    prow = 2 * 3 * wins * grp
    chunks = FREQ // LANE
    tail = chunks * rows

    barrier = pltpu.get_barrier_semaphore()

    def greet(k, carry):
        pl.semaphore_signal(barrier, inc=1, device_id={"pairs": (me + k) % owners},
                            device_id_type=pl.DeviceIdType.MESH)
        return carry

    lax.fori_loop(1, owners, greet, 0)

    pieces = []
    for a in range(3):
        seg = traces_ref[a].astype(f32)
        pieces += [seg[:, w * SEG:(w + 1) * SEG] for w in range(wins)]
    x = jnp.concatenate(pieces, axis=0).astype(bf16)
    spec = jnp.dot(x, dft_ref[...], preferred_element_type=f32)
    sq = spec * spec
    sq = sq[:, :FREQ] + sq[:, FREQ:]
    wi = wins * own
    power = (sq[:wi] + sq[wi:2 * wi] + sq[2 * wi:]) / 3.0
    wide = FREQ + LANE
    padded = jnp.concatenate([power, jnp.zeros((wi, LANE), f32)], axis=1)
    need, width, done, total, cur = 2 * HALF + 1, 1, 0, None, padded
    while width <= need:
        if need & width:
            term = cur if done == 0 else pltpu.roll(cur, done, 1)
            total = term if total is None else total + term
            done += width
        width *= 2
        if width <= need:
            cur = cur + pltpu.roll(cur, width // 2, 1)
    total = pltpu.roll(total, wide - HALF, 1)[:, :FREQ]
    col = lax.broadcasted_iota(jnp.int32, (wi, FREQ), 1)
    members = jnp.minimum(col + HALF, FREQ - 1) - jnp.maximum(col - HALF, 0) + 1
    smooth = total / members.astype(f32)
    row = lax.broadcasted_iota(jnp.int32, (wi, LANE), 0)
    flags = jnp.zeros((wi, LANE), f32)
    for w in range(wins):
        for i in range(own):
            flags = jnp.where(row == w * own + i, gaps_ref[w, i].astype(f32), flags)
    factor = jnp.concatenate([flags] * chunks, axis=1) / jnp.sqrt(smooth + 1e-6)
    white = jnp.concatenate(
        [spec[a * wi:(a + 1) * wi, p * FREQ:(p + 1) * FREQ] * factor for p in range(2) for a in range(3)], axis=0
    ).astype(bf16)
    for j in range(chunks):
        gath[me, j * rows:(j + 1) * rows] = white[:, j * LANE:(j + 1) * LANE]
    gath[me, tail:] = jnp.concatenate([flags, jnp.zeros((16 - wi, LANE), f32)], axis=0).astype(bf16)

    pl.semaphore_wait(barrier, owners - 1)

    def send(block, to, s_sem, r_sem):
        return pltpu.make_async_remote_copy(
            src_ref=gath.at[block], dst_ref=gath.at[block], send_sem=s_sem, recv_sem=r_sem,
            device_id={"pairs": to}, device_id_type=pl.DeviceIdType.MESH)

    def along(block, k):
        return send(block, (me + k * PLANE) % owners, zs.at[k], zr.at[k])

    def over(block, k):
        return send(block, across, ys.at[k], yr.at[k])

    def beside(block, k, half):
        return send(block, peer, cs.at[k, half], cr.at[k, half])

    def column(k):
        return (me - k * PLANE + owners) % owners

    def moved(block):
        return block + 2 - 4 * yy

    def turned(block):
        return block + 1 - 2 * core

    def send_own(k, carry):
        along(me, k).start()
        return carry

    lax.fori_loop(1, planes, send_own, 0)
    over(me, 0).start()
    beside(me, 0, 0).start()

    r_iota = lax.broadcasted_iota(jnp.int32, (prow, rows), 0)
    c_iota = lax.broadcasted_iota(jnp.int32, (prow, rows), 1)
    double = ((r_iota // grp == c_iota // own) & ((r_iota % grp) // CAP == c_iota % own))
    ownx[...] = jnp.dot(double.astype(f32).astype(bf16), white, preferred_element_type=f32)

    gr = lax.broadcasted_iota(jnp.int32, (grp, 16), 0)
    gc = lax.broadcasted_iota(jnp.int32, (grp, 16), 1)
    own_flags = jnp.zeros((grp, 16), f32)
    for w in range(wins):
        for i in range(own):
            own_flags = jnp.where((gr // CAP == i) & (gc // own == w), gaps_ref[w, i].astype(f32), own_flags)

    lane = lax.broadcasted_iota(jnp.int32, (grp, LANE), 1)

    def correlate(k):
        zg = (z - k + planes) % planes
        first = zg * PLANE
        base_r = lax.broadcasted_iota(jnp.int32, (prow, PLANE * rows), 0)
        base_c = lax.broadcasted_iota(jnp.int32, (prow, PLANE * rows), 1)
        odd = base_r % CAP == 1
        select, scales = [], []
        for j in range(PLANE):
            slots = pick(assign_ref, target_ref, first + j, me, own)
            station = jnp.where(odd, slots[1], slots[0])
            hit = (base_c // own == j * (rows // own) + base_r // grp) & (base_c % own == station)
            select.append(hit.astype(f32))
            station = jnp.where(gr % CAP == 1, slots[1], slots[0])
            weight = jnp.where(gc % own == station, own_flags, 0.0).astype(bf16)
            count = jnp.dot(weight, gath[first + j, tail:], preferred_element_type=f32)
            scales.append(1.0 / (jnp.maximum(count, 1.0) * math.sqrt(FREQ)))
        select = jnp.concatenate(select, axis=0).astype(bf16)
        data = jnp.concatenate(
            [
                jnp.concatenate([gath[first + j, n * rows:(n + 1) * rows] for n in range(chunks)], axis=1)
                for j in range(PLANE)
            ],
            axis=0,
        )
        part[...] = jnp.dot(select, data, preferred_element_type=f32)
        half = 3 * wins * grp
        for pair in range(PLANE // 2):
            for n in range(chunks):
                cols = slice(n * LANE, (n + 1) * LANE)
                for b in range(3):
                    for a in range(3):
                        res, ims = [], []
                        for par in range(2):
                            off = (pair * 2 + par) * prow
                            re = im = None
                            for w in range(wins):
                                oa = (a * wins + w) * grp
                                ob = off + (b * wins + w) * grp
                                wr, wm = ownx[oa:oa + grp, cols], ownx[half + oa:half + oa + grp, cols]
                                pr, pm = part[ob:ob + grp, cols], part[half + ob:half + ob + grp, cols]
                                r1, i1 = wr * pr + wm * pm, wm * pr - wr * pm
                                re, im = (r1, i1) if re is None else (re + r1, im + i1)
                            res.append(re)
                            ims.append(im)
                        at = (pair * 9 + 3 * a + b) * 2 * grp
                        cross[at:at + 2 * grp, cols] = jnp.concatenate(res, axis=0).astype(bf16)
                        cross[at:at + 2 * grp, FREQ + n * LANE:FREQ + (n + 1) * LANE] = (
                            jnp.concatenate(ims, axis=0).astype(bf16))
        lagged[...] = jnp.dot(cross[...], lag_ref[...], preferred_element_type=f32)
        for j in range(PLANE):
            e = first + j
            scale = jnp.concatenate([scales[j]] * (LAGS // LANE), axis=1)
            energies = jnp.zeros((grp, LANE), f32)
            for q in range(9):
                at = (((j // 2) * 9 + q) * 2 + j % 2) * grp
                value = (lagged[at:at + grp] * scale).astype(bf16)
                for i in range(own):
                    corr_ref[i, e, q] = value[CAP * i:CAP * (i + 1)]
                wide_value = value.astype(f32)
                energy = jnp.sum(wide_value * wide_value, axis=1, keepdims=True)
                energies = jnp.where(lane == q, energy, energies)
            esend[e] = energies

            @pl.when(e != me)
            def _():
                energy_copy(e, me).start()

            @pl.when(e == me)
            def _():
                erecv[me] = energies

    def energy_copy(to, source):
        return pltpu.make_async_remote_copy(
            src_ref=esend.at[to], dst_ref=erecv.at[source], send_sem=es.at[to], recv_sem=er.at[source],
            device_id={"pairs": to}, device_id_type=pl.DeviceIdType.MESH)

    def finish(k):
        block = column(k)
        over(moved(block), k).wait_recv()
        beside(moved(block), k, 1).start()
        beside(turned(block), k, 0).wait_recv()
        beside(turned(moved(block)), k, 1).wait_recv()
        correlate(k)

    finish(0)

    def forward(k, carry):
        block = column(k)
        along(block, k).wait_recv()
        over(block, k).start()
        beside(block, k, 0).start()
        return carry

    lax.fori_loop(1, planes, forward, 0)

    def rest(k, carry):
        finish(k)
        return carry

    lax.fori_loop(1, planes, rest, 0)

    cell = lax.broadcasted_iota(jnp.int32, (8, owners * grp), 1)
    chosen = jnp.full((8, owners * grp), -1, jnp.int32)

    def choose(p, chosen):
        slots = pick(assign_ref, target_ref, me, p, own)
        return jnp.where(cell // grp == p, jnp.where(cell % CAP == 1, slots[1], slots[0]), chosen)

    chosen = lax.fori_loop(0, owners, choose, chosen)
    pick_out = (chosen == lax.broadcasted_iota(jnp.int32, (8, owners * grp), 0)).astype(f32)

    def collect(k, carry):
        energy_copy(me, (me + k) % owners).wait_recv()
        return carry

    lax.fori_loop(1, owners, collect, 0)
    result = jnp.dot(pick_out, erecv[...].reshape(owners * grp, LANE),
                     precision=lax.Precision.HIGHEST, preferred_element_type=f32)
    energy_ref[...] = result[:own, :9] / float(owners * LAGS)

    def drain(k, carry):
        along(me, k).wait_send()
        return carry

    lax.fori_loop(1, planes, drain, 0)

    def drain_near(k, carry):
        over(me, k).wait_send()
        beside(me, k, 0).wait_send()
        beside(me, k, 1).wait_send()
        return carry

    lax.fori_loop(0, planes, drain_near, 0)

    def drain_energy(k, carry):
        energy_copy((me + k) % owners, me).wait_send()
        return carry

    lax.fori_loop(1, owners, drain_energy, 0)


def solution(mesh):
    owners = mesh.shape["pairs"]

    def on_device(traces, gaps, assign, target):
        own, wins = gaps.shape
        planes = owners // PLANE
        rows = 2 * 3 * wins * own
        grp = own * CAP
        dft, lag = tables()
        vmem = pl.BlockSpec(memory_space=pltpu.VMEM)
        smem = pl.BlockSpec(memory_space=pltpu.SMEM)
        dma = pltpu.SemaphoreType.DMA
        corr, energy = pl.pallas_call(
            functools.partial(kernel, owners, own, wins),
            out_shape=(
                jax.ShapeDtypeStruct((own, owners, 9, CAP, LAGS), jnp.bfloat16),
                jax.ShapeDtypeStruct((own, 9), jnp.float32),
            ),
            in_specs=[vmem, smem, smem, smem, vmem, vmem],
            out_specs=(vmem, vmem),
            scratch_shapes=[
                pltpu.VMEM((owners, (FREQ // LANE) * rows + 16, LANE), jnp.bfloat16),
                pltpu.VMEM((rows * CAP, FREQ), jnp.float32),
                pltpu.VMEM((PLANE * rows * CAP, FREQ), jnp.float32),
                pltpu.VMEM((PLANE * 9 * grp, 2 * FREQ), jnp.bfloat16),
                pltpu.VMEM((PLANE * 9 * grp, LAGS), jnp.float32),
                pltpu.VMEM((owners, grp, LANE), jnp.float32),
                pltpu.VMEM((owners, grp, LANE), jnp.float32),
                dma((planes,)), dma((planes,)), dma((planes,)), dma((planes,)),
                dma((planes, 2)), dma((planes, 2)), dma((owners,)), dma((owners,)),
            ],
            compiler_params=pltpu.CompilerParams(
                collective_id=0, has_side_effects=True, vmem_limit_bytes=48 * 1024 * 1024),
        )(traces.transpose(1, 0, 2), gaps.T, assign, target, dft, lag)
        return corr.transpose(0, 1, 3, 2, 4), energy

    in_specs = (
        P(("groups", "pairs"), None, None),
        P(("groups", "pairs"), None),
        P("groups"),
        P("groups"),
    )
    out_specs = (P(("groups", "pairs"), None, None, None, None), P(("groups", "pairs"), None))
    return jax.shard_map(
        on_device, mesh=mesh, in_specs=in_specs, out_specs=out_specs, check_vma=False
    )
```

time: 123 us -> 33.8 us (0.27)
  blocking collectives: 42.8 us -> 0 us
  Pallas kernels: 0 us -> 25.4 us
  local copies, waits for them, and re-layouts: 31.3 us -> 7.5 us
  other arithmetic: 21.9 us -> 0 us
  matrix products: 17.3 us -> 0 us
  waiting for transfers between devices: 4.72 us -> 0 us
  starting transfers between devices: 3.49 us -> 0 us
    all_gather x2 -> x0, blocking collectives: 42.8 us -> none  [the longest x1 25.5 us: on_device(): lax.all_gather(station_rows, 'pairs', axis=0, tiled=True)]
    pallas_call x0 -> x1, Pallas kernels: none -> 25.4 us  [on_device(): pl.pallas_call(functools.partial(kernel, owners, own, wins), out_shape=(j...]
    another operation x3 -> x0, other arithmetic: 20.2 us -> none
    dot_general x8 -> x0, matrix products: 17.3 us -> none  [the longest x1 11.5 us: correlate_block(): jnp.einsum('icwrf,jdwrof->ijcdof', whitened, quad, preferred_element_type...]
    convert_element_type x2 -> x0, local copies, waits for them, and re-layouts: 16.1 us -> none  [the longest x1 14.3 us: correlate_block(): cross = cross.astype(jnp.bfloat16)]
    another operation x3 -> x0, local copies, waits for them, and re-layouts: 6.85 us -> none  [the longest x1 3.52 us: correlate_block(): jnp.stack([-imag_part, real_part], 3)]
    unnamed x15 -> x14, local copies, waits for them, and re-layouts: 2.3 us -> 7.5 us
    all_to_all x1 -> x0, waiting for transfers between devices: 4.72 us -> none  [on_device(): lax.all_to_all(slot_energy, 'pairs', split_axis=0, concat_axis=0, tiled=T...]
  transfers between devices with their start and end apart: 1 -> 0, of which waited for: 1 -> 0; matrix products, arithmetic and copies ran while one was open for 1% -> 0% of each run, Pallas kernels for 0% -> 0%
where the time goes in v1:
time: 33.8 us; the launch traced here: 33.6 us
  Pallas kernels  25.4 us (75%)
  local copies, waits for them, and re-layouts  7.5 us (22%)
  between operations  0.65 us (2%)
    pallas_call x1, Pallas kernels, on_device(): pl.pallas_call(functools.partial(kernel, owners, own, wins), out_shape=(j...  25.4 us
    unnamed x14, local copies, waits for them, and re-layouts  7.5 us

profile of v1, /device:TPU:0, one launch (start us, length us, event | category | flops | bytes accessed | tf_op | source)
XLA Modules:
  0.0 33.6 jit_solution(3703092533891521342)
XLA Ops:
  0.6 0.0 copy-start
  0.6 2.2 %copy-done = bf16[2048,1024]{1,0:T(8,128)(2,1)S(1)} copy-done((bf16[2048,1024]{1,0:T(8,128)(2,1)S(1)}, bf16[2048,1024]{1,0:T(8,128)(2,1)}, u32[]{:S(2)}) %copy-start) | copy-done | bytes 4194328
  2.8 0.0 copy-start.1
  2.8 1.0 %copy-done.1 = bf16[1024,256]{1,0:T(8,128)(2,1)S(1)} copy-done((bf16[1024,256]{1,0:T(8,128)(2,1)S(1)}, bf16[1024,256]{1,0:T(8,128)(2,1)}, u32[]{:S(2)}) %copy-start.1) | copy-done | bytes 524312
  3.9 0.0 copy-start.2
  3.9 0.9 %copy-done.2 = bf16[4,3,4096]{2,0,1:T(4,128)(2,1)S(1)} copy-done((bf16[4,3,4096]{2,0,1:T(4,128)(2,1)S(1)}, bf16[4,3,4096]{2,0,1:T(4,128)(2,1)}, u32[]{:S(2)}) %copy-start.2) | copy-done | bytes 98328
  4.8 0.0 copy-start.3
  4.8 0.7 %copy-done.3 = s32[4,2]{0,1:T(2,128)S(1)} copy-done((s32[4,2]{0,1:T(2,128)S(1)}, s32[4,2]{0,1:T(2,128)}, u32[]{:S(2)}) %copy-start.3) | copy-done | bytes 56
  5.4 0.0 copy-start.4
  5.4 0.7 %copy-done.4 = s32[64]{0:T(128)S(1)} copy-done((s32[64]{0:T(128)S(1)}, s32[64]{0:T(128)}, u32[]{:S(2)}) %copy-start.4) | copy-done | bytes 280
  6.1 0.0 copy-start.5
  6.1 0.7 %copy-done.5 = s32[16]{0:T(128)S(1)} copy-done((s32[16]{0:T(128)S(1)}, s32[16]{0:T(128)}, u32[]{:S(2)}) %copy-start.5) | copy-done | bytes 88
  6.7 25.4 %shard_map.77 = (bf16[4,16,9,2,256]{4,3,2,1,0:T(2,128)(2,1)S(1)}, f32[4,9]{1,0:T(4,128)S(1)}) custom-call(bf16[3,4,4096]{2,1,0:T(4,128)(2,1)S(1)} %bitcast.4, s32[2,4]{1,0:T(2,128)S(1)} %bitcast.5, s32[64]{0:T(128)S(1)} %copy-done.4, s32[16]{0:T(128)S(1)} %copy-done.5, bf16[2048,1024]{1,0:T(8,128)(2,1)S(1)} %copy-done, bf16[1024,256]{1,0:T(8,128)(2,1)S(1)} %copy-done.1), custom_call_target="tpu_custom_call" | custom-call | tf_op jit(solution)/shard_map/pallas_call | solution.py:312
  32.2 0.8 %copy.10 = bf16[4,16,2,9,256]{4,2,3,1,0:T(2,128)(2,1)} copy(bf16[4,16,2,9,256]{4,2,3,1,0:T(2,128)(2,1)S(1)} %bitcast.3) | data formatting | bytes 1179648
  33.0 0.6 %copy.11 = f32[4,9]{1,0:T(4,128)} copy(f32[4,9]{1,0:T(4,128)S(1)} %get-tuple-element.9) | data formatting | bytes 288
Async XLA Ops:
  0.6 2.2 %copy-start = (bf16[2048,1024]{1,0:T(8,128)(2,1)S(1)}, bf16[2048,1024]{1,0:T(8,128)(2,1)}, u32[]{:S(2)}) copy-start(bf16[2048,1024]{1,0:T(8,128)(2,1)} %constant.4.clone.dft_ref) | copy-start | bytes 12582916
  2.8 1.0 %copy-start.1 = (bf16[1024,256]{1,0:T(8,128)(2,1)S(1)}, bf16[1024,256]{1,0:T(8,128)(2,1)}, u32[]{:S(2)}) copy-start(bf16[1024,256]{1,0:T(8,128)(2,1)} %constant.5.clone.lag_ref) | copy-start | bytes 1572868
  3.9 0.9 %copy-start.2 = (bf16[4,3,4096]{2,0,1:T(4,128)(2,1)S(1)}, bf16[4,3,4096]{2,0,1:T(4,128)(2,1)}, u32[]{:S(2)}) copy-start(bf16[4,3,4096]{2,0,1:T(4,128)(2,1)} %param.6) | copy-start | bytes 294916
  4.8 0.7 %copy-start.3 = (s32[4,2]{0,1:T(2,128)S(1)}, s32[4,2]{0,1:T(2,128)}, u32[]{:S(2)}) copy-start(s32[4,2]{0,1:T(2,128)} %param.7) | copy-start | bytes 100
  5.4 0.7 %copy-start.4 = (s32[64]{0:T(128)S(1)}, s32[64]{0:T(128)}, u32[]{:S(2)}) copy-start(s32[64]{0:T(128)} %assign_ref.1) | copy-start | bytes 772
  6.1 0.7 %copy-start.5 = (s32[16]{0:T(128)S(1)}, s32[16]{0:T(128)}, u32[]{:S(2)}) copy-start(s32[16]{0:T(128)} %target_ref.1) | copy-start | bytes 196
